TPU v7x, 128 devices: a whole 4x4x4 slice. The times are simulated.
128 devices in a mesh: rows: 32 (over x, z, y_hi), cols: 4 (over y_lo, core).
Axes of the slice: x: 4, y: 4 (y_hi: 2, y_lo: 2; y = y_hi * 2 + y_lo), z: 4, core: 2. Of those that a mesh axis runs over, the one named last changes fastest.
Arguments:
- snapshots: float32 [64, 2, 512, 512], P('cols', None, 'rows'), may hold values from -6 to 6
- adjoint: bfloat16 [2048, 2, 512, 512], P('cols', None, 'rows'), may hold values from -0.0078125 to 0.0078125
- base_flow: float32 [512], replicated, may hold values from 0.3 to 1
- shear: float32 [512], replicated, may hold values from -1 to 1
Outputs:
- advanced: float32 [64, 2, 512, 512], P('cols', None, 'rows')
- gram: float32 [2, 64, 2048], P(None, None, 'cols')
All inputs are finite; a program needn't handle non-finite values.
Results may differ from a plain program's by a relative error of at most 0.0031.
Values may be sent and summed in bfloat16 or wider, within the bound.
A program may use at most 128 MiB of HBM per device.

v0:
```python
import jax
import jax.numpy as jnp
from jax import lax
from jax.sharding import PartitionSpec as P


def padded_2(cells, sides, width):
    for axis, dim in sides:
        count = lax.axis_size(axis)
        head = lax.slice_in_dim(cells, 0, width, axis=dim)
        tail = lax.slice_in_dim(cells, cells.shape[dim] - width, cells.shape[dim], axis=dim)
        cells = jnp.concatenate(
            [
                lax.ppermute(tail, axis, [(i, (i + 1) % count) for i in range(count)]),
                cells,
                lax.ppermute(head, axis, [((i + 1) % count, i) for i in range(count)]),
            ],
            axis=dim,
        )
    return cells


def advance(padded, base_flow, shear):
    field = padded[:, :, 1:-1]
    ahead = padded[:, :, 2:]
    behind = padded[:, :, :-2]
    walled = jnp.pad(field, ((0, 0), (0, 0), (0, 0), (1, 1)))
    laplace = ahead + behind + walled[..., 2:] + walled[..., :-2] - 4.0 * field
    result = field + 0.1 * laplace - 0.3 * base_flow * (ahead - behind)
    coupling = 0.3 * shear * field[:, 1]
    return result.at[:, 0].add(-coupling)


def per_device(snapshots, adjoint, base_flow, shear):
    adjoint_flat = adjoint.reshape(adjoint.shape[0], -1)

    def project(piece):
        return jnp.dot(piece, adjoint_flat.T, preferred_element_type=jnp.float32)

    local_snaps = snapshots.shape[0]

    def single(field):
        return padded_2(field, (("rows", 2),), 1)

    state_one = advance(single(snapshots), base_flow, shear)
    advanced = None
    low_one = state_one.astype(jnp.bfloat16).reshape(local_snaps, -1)
    first = project(lax.all_gather(low_one, "cols", axis=0, tiled=True))
    advanced = advance(single(state_one), base_flow, shear)
    low_two = advanced.astype(jnp.bfloat16).reshape(local_snaps, -1)
    second = project(lax.all_gather(low_two, "cols", axis=0, tiled=True))
    partial_value = jnp.stack([first, second])
    gram = lax.psum(partial_value, "rows")
    return (advanced, gram)


def solution(mesh):
    in_specs = (P("cols", None, "rows", None), P("cols", None, "rows", None), P(), P())
    out_specs = (P("cols", None, "rows", None), P(None, None, "cols"))
    return jax.shard_map(
        per_device, mesh=mesh, in_specs=in_specs, out_specs=out_specs, check_vma=False
    )
```

profile of v0, /device:TPU:0, one launch (start us, length us, event | category | flops | bytes accessed | tf_op | source)
XLA Modules:
  0.0 468.7 jit_solution(2507398578684221255)
XLA Ops:
  7.2 1.4 fusion.18
  8.6 9.0 %collective-permute-start = (f32[16,2,1,512]{3,2,1,0:T(1,128)S(1)}, f32[16,2,1,512]{3,2,1,0:T(1,128)S(1)}, u32[]{:S(2)}, u32[]{:S(2)}) collective-permute-start(f32[16,2,1,512]{3,2,1,0:T(1,128)S(1)} %get-tuple-element.31), channel_id=1, source_target_pairs={{4,0},{8,4},{12,8},{16,12},{20,16},{24,20},{28,24},{32,28},{36,32}... | collective-permute-start | bytes 196616 | tf_op jit(solution)/shard_map/ppermute | solution.py:16
  17.6 0.7 broadcast_multiply_fusion.1
  18.3 0.7 broadcast_multiply_fusion
  19.0 0.5 collective-permute-done
  19.5 8.1 %collective-permute-done.1 = f32[16,2,1,512]{3,2,1,0:T(1,128)S(1)} collective-permute-done((f32[16,2,1,512]{3,2,1,0:T(1,128)S(1)}, f32[16,2,1,512]{3,2,1,0:T(1,128)S(1)}, u32[]{:S(2)}, u32[]{:S(2)}) %collective-permute-start.1) | collective-permute-done | bytes 65568 | tf_op jit(solution)/shard_map/ppermute | solution.py:14
  27.6 3.7 fusion.5
  31.3 0.2 fusion.15
  31.8 3.5 collective-permute-start.3
  35.3 2.2 collective-permute-done.2
  37.5 4.3 collective-permute-done.3
  41.8 0.9 fusion.16
  42.7 0.2 fusion.14
  43.0 1.1 copy.8
  44.1 1.1 copy.6
  45.3 0.2 all-reduce.4.cloned.1.call-start
  45.5 18.6 %copy.7 = bf16[64,8,32,512]{3,1,2,0:T(8,128)(2,1)} copy(bf16[64,8,32,512]{3,2,1,0:T(8,128)(2,1)} %bitcast.19) | data formatting | bytes 33554432
  64.0 3.1 all-gather.5.cloned.1.call-done
  67.1 11.6 %convolution_bitcast_fusion = f32[1,64,512]{2,1,0:T(8,128)S(1)} fusion(bf16[64,16384]{1,0:T(8,128)(2,1)} %all-gather.5.cloned.1.call-done, bf16[512,16384]{1,0:T(8,128)(2,1)} %bitcast.17), kind=kOutput, calls=%fused_computation.4 | convolution fusion | flops 1073741824 | bytes 19005440 | tf_op jit(solution)/shard_map/dot_general | solution.py:38
  78.7 20.1 %all-gather.3.cloned.1.call-done = bf16[64,16384]{1,0:T(8,128)(2,1)} async-done(((bf16[16,16384]{1,0:T(8,128)(2,1)}), bf16[64,16384]{1,0:T(8,128)(2,1)}) %all-gather.3.cloned.1.call-update) | async-done | bytes 2097168 | tf_op jit(solution)/shard_map/all_gather | solution.py:48
  98.8 11.6 %convolution_bitcast_fusion.1 = f32[1,64,512]{2,1,0:T(8,128)S(1)} fusion(bf16[64,16384]{1,0:T(8,128)(2,1)} %all-gather.3.cloned.1.call-done, bf16[512,16384]{1,0:T(8,128)(2,1)} %bitcast.18), kind=kOutput, calls=%fused_computation.5 | convolution fusion | flops 1073741824 | bytes 19005440 | tf_op jit(solution)/shard_map/dot_general | solution.py:38
  110.4 0.7 pad_maximum_fusion.4
  111.1 349.4 %all-reduce.4.cloned.1.call-done = f32[2,64,512]{2,1,0:T(8,128)} async-done(((f32[2,64,512]{2,1,0:T(8,128)}), f32[2,64,512]{2,1,0:T(8,128)}) %all-reduce.4.cloned.1.call-update) | async-done | bytes 262160 | tf_op jit(solution)/shard_map/psum | solution.py:53
  460.5 1.7 copy.12
  (13 shorter events, 0.4 us)
Async XLA Ops:
  7.2 24.2 %copy-start.1 = (f32[16,2,16,512]{3,2,1,0:T(8,128)S(1)}, f32[16,2,16,512]{3,2,1,0:T(8,128)}, u32[]{:S(2)}) copy-start(f32[16,2,16,512]{3,2,1,0:T(8,128)} %param.8) | copy-start | bytes 3145732
  7.2 59.9 %all-gather.5.cloned.1.call-start = ((), (), s32[]{:S(2)}) async-start(), calls=%async_computation.1 | async-start | bytes 2621440 | tf_op jit(solution)/shard_map/all_gather | solution.py:51
  8.6 10.9 %collective-permute-start = (f32[16,2,1,512]{3,2,1,0:T(1,128)S(1)}, f32[16,2,1,512]{3,2,1,0:T(1,128)S(1)}, u32[]{:S(2)}, u32[]{:S(2)}) collective-permute-start(f32[16,2,1,512]{3,2,1,0:T(1,128)S(1)} %get-tuple-element.31), channel_id=1, source_target_pairs={{4,0},{8,4},{12,8},{16,12},{20,16},{24,20},{28,24},{32,28},{36,32}... | collective-permute-start | bytes 196616 | tf_op jit(solution)/shard_map/ppermute | solution.py:16
  17.6 10.0 %collective-permute-start.1 = (f32[16,2,1,512]{3,2,1,0:T(1,128)S(1)}, f32[16,2,1,512]{3,2,1,0:T(1,128)S(1)}, u32[]{:S(2)}, u32[]{:S(2)}) collective-permute-start(f32[16,2,1,512]{3,2,1,0:T(1,128)S(1)} %get-tuple-element.30), channel_id=1, source_target_pairs={{0,4},{4,8},{8,12},{12,16},{16,20},{20,24},{24,28},{28,32},{32,36}... | collective-permute-start | bytes 196616 | tf_op jit(solution)/shard_map/ppermute | solution.py:14
  31.7 5.8 %collective-permute-start.2 = (f32[16,2,1,512]{3,2,1,0:T(1,128)S(1)}, f32[16,2,1,512]{3,2,1,0:T(1,128)S(1)}, u32[]{:S(2)}, u32[]{:S(2)}) collective-permute-start(f32[16,2,1,512]{3,2,1,0:T(1,128)S(1)} %get-tuple-element.29), channel_id=1, source_target_pairs={{4,0},{8,4},{12,8},{16,12},{20,16},{24,20},{28,24},{32,28},{36,32}... | collective-permute-start | bytes 196616 | tf_op jit(solution)/shard_map/ppermute | solution.py:16
  31.8 10.1 %collective-permute-start.3 = (f32[16,2,1,512]{3,2,1,0:T(1,128)S(1)}, f32[16,2,1,512]{3,2,1,0:T(1,128)S(1)}, u32[]{:S(2)}, u32[]{:S(2)}) collective-permute-start(f32[16,2,1,512]{3,2,1,0:T(1,128)S(1)} %get-tuple-element.28), channel_id=1, source_target_pairs={{0,4},{4,8},{8,12},{12,16},{16,20},{20,24},{24,28},{28,32},{32,36}... | collective-permute-start | bytes 196616 | tf_op jit(solution)/shard_map/ppermute | solution.py:14
  42.9 2.4 copy-start
  44.1 54.7 %all-gather.3.cloned.1.call-start = ((), (), s32[]{:S(2)}) async-start(), calls=%async_computation | async-start | bytes 2621440 | tf_op jit(solution)/shard_map/all_gather | solution.py:48
  45.3 415.3 %all-reduce.4.cloned.1.call-start = ((), (), s32[]{:S(2)}) async-start(), calls=%async_computation.2 | async-start | bytes 524288 | tf_op jit(solution)/shard_map/psum | solution.py:53
Sparse Core Ops, SparseCore 0:
  44.2 22.8 all-gather.4
  68.8 29.9 all-gather.2
  111.2 349.2 all-reduce.3
where the time goes:
time: 469 us
  waiting for transfers between devices  388 us (83%)
  local copies, waits for them, and re-layouts  23.9 us (5%)
  matrix products  23.2 us (5%)
  between operations  13.8 us (3%)
  starting transfers between devices  12.9 us (3%)
  other arithmetic  7.14 us (2%)
    psum x1, waiting for transfers between devices, per_device(): gram = lax.psum(partial_value, 'rows')  349 us
    dot_general x2, matrix products, project(): return jnp.dot(piece, adjoint_flat.T, preferred_element_type=jnp.float32)  23.2 us
    unnamed x8, local copies, waits for them, and re-layouts  22.4 us
    all_gather x1, waiting for transfers between devices, per_device(): first = project(lax.all_gather(low_one, 'cols', axis=0, tiled=True))  20.1 us
    ppermute x2, waiting for transfers between devices, padded_2(): lax.ppermute(tail, axis, [(i, (i + 1) % count) for i in range(count)])  12.4 us
  transfers between devices with their start and end apart: 7, of which 7 were waited for; matrix products, arithmetic and copies ran while one was open for 7% of the time, Pallas kernels for 0%

commit v1 on v0

v1 whole, which is shorter than its diff:
```python
import functools

import jax
import jax.numpy as jnp
from jax import lax
from jax.experimental import pallas as pl
from jax.experimental.pallas import tpu as pltpu
from jax.sharding import PartitionSpec as P

ROWS = 32
SNAPS = 16
ADJS = 512
NX = 16
NY = 512
BLOCK = 32
LOADS = ADJS // BLOCK
RING = 8
SCALE = 8192.0
TINY = 1e-37
CUTS = ((2, 6), (8, 4), (12, 4), (16, 2))
MESH = pl.DeviceIdType.MESH
NT = (((1,), (1,)), ((), ()))
F32 = jnp.float32
LOW = jnp.bfloat16


def encode(value):
    scaled = value * SCALE
    square = scaled * scaled
    return ((scaled * jnp.abs(scaled)) * (square * (square * square))).astype(LOW)


def decode(code):
    wide = code.astype(F32)
    half = lax.rsqrt(jnp.maximum(jnp.abs(wide), TINY))
    eighth = lax.rsqrt(lax.rsqrt(half))
    return (wide * half) * (eighth * eighth * eighth) * (1.0 / SCALE)


def kernel(
    snaps_hbm, adj_hbm, base_ref, shear_ref,
    adv_hbm, gram_ref,
    snaps, coef, own, own_one, own_adv, adv_out, code, far_code, far, far_one,
    low, adj_raw, adj, total, part, gather, result,
    io_sem, load_sem, halo_send, halo_recv, far_send, far_recv,
    pass_send, pass_recv, side_send, side_recv, sum_sem,
):
    row = lax.axis_index("rows")
    col = lax.axis_index("cols")
    core = col % 2
    side = col + 1 - 2 * core
    far_col = (col + 2) % 4
    up = (row + 1) % ROWS
    down = (row + ROWS - 1) % ROWS

    def load(i):
        return pltpu.make_async_copy(
            adj_hbm.at[pl.ds(pl.multiple_of(i * BLOCK, BLOCK), BLOCK)],
            adj_raw.at[i % RING],
            load_sem.at[i % RING],
        )

    snaps_in = pltpu.make_async_copy(snaps_hbm, snaps, io_sem.at[0])
    snaps_in.start()
    for i in range(RING):
        load(i).start()

    barrier = pltpu.get_barrier_semaphore()
    pl.semaphore_signal(barrier, inc=1, device_id=(row, far_col), device_id_type=MESH)
    pl.semaphore_signal(barrier, inc=1, device_id=(row, side), device_id_type=MESH)
    pl.semaphore_signal(barrier, inc=1, device_id=(up, far_col), device_id_type=MESH)
    pl.semaphore_signal(barrier, inc=1, device_id=(down, far_col), device_id_type=MESH)

    def greet(d, _):
        pl.semaphore_signal(
            barrier, inc=1, device_id=((row + d) % ROWS, col), device_id_type=MESH
        )
        return 0

    lax.fori_loop(1, ROWS, greet, 0)

    lane = lax.broadcasted_iota(jnp.int32, (SNAPS, NY), 1)
    base = jnp.broadcast_to(base_ref[...], (SNAPS, NY))
    coef[0] = 0.1 - 0.3 * base
    coef[1] = 0.1 + 0.3 * base
    coef[2] = jnp.where(lane == NY - 1, 0.0, 0.1)
    coef[3] = jnp.where(lane == 0, 0.0, 0.1)
    coef[4] = 0.3 * jnp.broadcast_to(shear_ref[...], (SNAPS, NY))

    snaps_in.wait()
    for c in range(2):
        turned = jnp.swapaxes(snaps[:, c], 0, 1)
        own[pl.ds(2, NX), c] = turned
        code[:, c] = encode(turned)

    pl.semaphore_wait(barrier, ROWS - 1 + 4)

    halos = []
    for i, (to_row, to_col) in enumerate(
        ((up, col), (down, col), (up, far_col), (down, far_col))
    ):
        src = code.at[pl.ds(NX - 2, 2)] if i % 2 == 0 else code.at[pl.ds(0, 2)]
        at = 0 if i % 2 == 0 else NX + 2
        if i < 2:
            dst = own_halo(far_code, at)
        else:
            dst = far_code.at[pl.ds(at, 2), :, pl.ds(pl.multiple_of(core * SNAPS, SNAPS), SNAPS)]
        halos.append(
            pltpu.make_async_remote_copy(
                src, dst, halo_send.at[i], halo_recv.at[i],
                device_id=(to_row, to_col), device_id_type=MESH,
            )
        )
    fars = []
    for j, (at, count) in enumerate(CUTS):
        fars.append(
            pltpu.make_async_remote_copy(
                code.at[pl.ds(at - 2, count)],
                far_code.at[pl.ds(at, count), :, pl.ds(pl.multiple_of(core * SNAPS, SNAPS), SNAPS)],
                far_send.at[j], far_recv.at[j],
                device_id=(row, far_col), device_id_type=MESH,
            )
        )
    for copy in halos:
        copy.start()
    for copy in fars:
        copy.start()

    def passing(k, at, count):
        piece = far_code.at[pl.ds(at, count), :, pl.ds(pl.multiple_of(core * SNAPS, SNAPS), SNAPS)]
        return pltpu.make_async_remote_copy(
            piece, piece, pass_send.at[k], pass_recv.at[k],
            device_id=(row, side), device_id_type=MESH,
        )

    passes = [passing(j, at, count) for j, (at, count) in enumerate(CUTS)]
    passes += [passing(4, 0, 2), passing(5, NX + 2, 2)]

    def turn(i, _):
        load(i).wait()
        for c in range(2):
            block = jnp.swapaxes(adj_raw[i % RING, :, c], 0, 1)
            for x in range(NX):
                adj[2 * x + c, pl.ds(pl.multiple_of(i * BLOCK, BLOCK), BLOCK)] = block[x]

        @pl.when(i + RING < LOADS)
        def _():
            load(i + RING).start()

        return 0

    def step(read, x):
        result = []
        flow = [read(x, 0), read(x, 1)]
        for c in range(2):
            here = flow[c]
            value = 0.6 * here
            value += coef[0] * read(x + 1, c) + coef[1] * read(x - 1, c)
            value += coef[2] * pltpu.roll(here, NY - 1, 1) + coef[3] * pltpu.roll(here, 1, 1)
            if c == 0:
                value -= coef[4] * flow[1]
            result.append(value)
        return result

    lax.fori_loop(0, LOADS // 2, turn, 0)

    for i in range(2):
        halos[i].wait_recv()
        at = 0 if i == 0 else NX + 2
        for k in range(2):
            for c in range(2):
                own[at + k, c] = decode(own_halo(far_code, at)[k, c])

    own_at = pl.multiple_of(col * SNAPS, SNAPS)

    def own_first(x, _):
        values = step(lambda k, c: own[k + 1, c], x)
        for c in range(2):
            own_one[x, c] = values[c]
        return 0

    lax.fori_loop(0, NX + 2, own_first, 0)

    def own_second(x, _):
        values = step(lambda k, c: own_one[k + 1, c], x)
        for c in range(2):
            own_adv[x, c] = values[c]
            low[2 * x + c, pl.ds(own_at, SNAPS)] = own_one[x + 1, c].astype(LOW)
            low[2 * x + c, pl.ds(own_at + 64, SNAPS)] = values[c].astype(LOW)
        return 0

    lax.fori_loop(0, NX, own_second, 0)

    sides = []
    for k in range(2):
        piece = low.at[:, pl.ds(own_at + 64 * k, SNAPS)]
        sides.append(
            pltpu.make_async_remote_copy(
                piece, piece, side_send.at[k], side_recv.at[k],
                device_id=(row, side), device_id_type=MESH,
            )
        )
    for copy in sides:
        copy.start()

    for k in range(2):
        halos[2 + k].wait_recv()
        passes[4 + k].start()
    fars[0].wait_recv()
    passes[0].start()

    lax.fori_loop(LOADS // 2, LOADS, turn, 0)

    for c in range(2):
        adv_out[:, c] = jnp.swapaxes(own_adv[:, c], 0, 1)
    adv_copy = pltpu.make_async_copy(adv_out, adv_hbm, io_sem.at[1])
    adv_copy.start()

    far_at = pl.multiple_of(((col // 2 + 1) % 2) * 32, 32)

    def states(part_at, first, count, x_one, n_one, x_two):
        at = pl.multiple_of(part_at * SNAPS, SNAPS)

        def widen(k, _):
            for c in range(2):
                far[k, c, pl.ds(at, SNAPS)] = decode(far_code[k, c, pl.ds(at, SNAPS)])
            return 0

        lax.fori_loop(first, first + count, widen, 0)

        def one(x, _):
            values = step(lambda k, c: far[k + 1, c, pl.ds(at, SNAPS)], x)
            for c in range(2):
                far_one[x, c, pl.ds(at, SNAPS)] = values[c]
            return 0

        lax.fori_loop(x_one, x_one + n_one, one, 0)
        low_at = pl.multiple_of(far_at + at, SNAPS)

        def two(x, _):
            values = step(lambda k, c: far_one[k + 1, c, pl.ds(at, SNAPS)], x)
            for c in range(2):
                low[2 * x + c, pl.ds(low_at, SNAPS)] = far_one[x + 1, c, pl.ds(at, SNAPS)].astype(LOW)
                low[2 * x + c, pl.ds(low_at + 64, SNAPS)] = values[c].astype(LOW)
            return 0

        lax.fori_loop(x_two, x_two + 4, two, 0)

    def multiply(j):
        def body(k, _):
            at = 8 * j + 4 * k
            left = jnp.concatenate([low[at + i] for i in range(4)], axis=1)
            right = jnp.concatenate([adj[at + i] for i in range(4)], axis=1)
            total[...] += lax.dot_general(left, right, NT, preferred_element_type=F32)
            return 0

        lax.fori_loop(0, 2, body, 0)

    total[...] = jnp.zeros((128, ADJS), F32)
    for j in range(4):
        if j > 0:
            fars[j].wait_recv()
            passes[j].start()
        first, count = (0, 8) if j == 0 else (4 * j + 4, 4)
        x_one, n_one = (0, 6) if j == 0 else (4 * j + 2, 4)
        states(core, first, count, x_one, n_one, 4 * j)
        if j == 0:
            passes[4].wait_recv()
            passes[5].wait_recv()
            sides[0].wait_recv()
            sides[1].wait_recv()
        passes[j].wait_recv()
        states(1 - core, first, count, x_one, n_one, 4 * j)
        multiply(j)

    for t in range(ROWS):
        part[t] = total[pl.ds(16 * (t // 4), 16), pl.ds(128 * (t % 4), 128)]

    def scatter(d, _):
        to = (row + d) % ROWS
        pltpu.make_async_remote_copy(
            part.at[to], gather.at[row], sum_sem.at[0], sum_sem.at[1],
            device_id=(to, col), device_id_type=MESH,
        ).start()
        return 0

    lax.fori_loop(1, ROWS, scatter, 0)
    gather[row] = part[row]
    others = gather.at[pl.ds(0, ROWS - 1)]
    pltpu.make_async_copy(others, others, sum_sem.at[1]).wait()
    piece = gather[0]
    for t in range(1, ROWS):
        piece = piece + gather[t]
    result[row] = piece

    def spread(d, _):
        to = (row + d) % ROWS
        pltpu.make_async_remote_copy(
            result.at[row], result.at[row], sum_sem.at[2], sum_sem.at[3],
            device_id=(to, col), device_id_type=MESH,
        ).start()
        return 0

    lax.fori_loop(1, ROWS, spread, 0)
    adv_copy.wait()
    for copy in halos + fars + passes + sides:
        copy.wait_send()
    pltpu.make_async_copy(others, others, sum_sem.at[0]).wait()
    pltpu.make_async_copy(others, others, sum_sem.at[3]).wait()
    for t in range(ROWS):
        at = 16 * (t // 4)
        gram_ref[at // 64, pl.ds(at % 64, 16), pl.ds(128 * (t % 4), 128)] = result[t]
    pltpu.make_async_copy(others, others, sum_sem.at[2]).wait()


def own_halo(ref, at):
    return ref.at[pl.ds(NX + 4 + (0 if at == 0 else 2), 2), :, pl.ds(0, SNAPS)]


def per_device(snapshots, adjoint, base_flow, shear):
    vmem = pltpu.VMEM
    return pl.pallas_call(
        kernel,
        out_shape=(
            jax.ShapeDtypeStruct((SNAPS, 2, NX, NY), F32),
            jax.ShapeDtypeStruct((2, 64, ADJS), F32),
        ),
        in_specs=[
            pl.BlockSpec(memory_space=pl.ANY),
            pl.BlockSpec(memory_space=pl.ANY),
            pl.BlockSpec(memory_space=vmem),
            pl.BlockSpec(memory_space=vmem),
        ],
        out_specs=(pl.BlockSpec(memory_space=pl.ANY), pl.BlockSpec(memory_space=vmem)),
        scratch_shapes=[
            vmem((SNAPS, 2, NX, NY), F32),
            vmem((5, SNAPS, NY), F32),
            vmem((NX + 4, 2, SNAPS, NY), F32),
            vmem((NX + 2, 2, SNAPS, NY), F32),
            vmem((NX, 2, SNAPS, NY), F32),
            vmem((SNAPS, 2, NX, NY), F32),
            vmem((NX, 2, SNAPS, NY), LOW),
            vmem((NX + 8, 2, 2 * SNAPS, NY), LOW),
            vmem((NX + 4, 2, 2 * SNAPS, NY), F32),
            vmem((NX + 2, 2, 2 * SNAPS, NY), F32),
            vmem((2 * NX, 128, NY), LOW),
            vmem((RING, BLOCK, 2, NX, NY), LOW),
            vmem((2 * NX, ADJS, NY), LOW),
            vmem((128, ADJS), F32),
            vmem((ROWS, 16, 128), F32),
            vmem((ROWS, 16, 128), F32),
            vmem((ROWS, 16, 128), F32),
            pltpu.SemaphoreType.DMA((2,)),
            pltpu.SemaphoreType.DMA((RING,)),
            pltpu.SemaphoreType.DMA((4,)),
            pltpu.SemaphoreType.DMA((4,)),
            pltpu.SemaphoreType.DMA((4,)),
            pltpu.SemaphoreType.DMA((4,)),
            pltpu.SemaphoreType.DMA((6,)),
            pltpu.SemaphoreType.DMA((6,)),
            pltpu.SemaphoreType.DMA((2,)),
            pltpu.SemaphoreType.DMA((2,)),
            pltpu.SemaphoreType.DMA((4,)),
        ],
        compiler_params=pltpu.CompilerParams(
            collective_id=0, has_side_effects=True, vmem_limit_bytes=60 * 2**20
        ),
    )(snapshots, adjoint, base_flow.reshape(1, NY), shear.reshape(1, NY))


def solution(mesh):
    in_specs = (P("cols", None, "rows", None), P("cols", None, "rows", None), P(), P())
    out_specs = (P("cols", None, "rows", None), P(None, None, "cols"))
    return jax.shard_map(
        per_device, mesh=mesh, in_specs=in_specs, out_specs=out_specs, check_vma=False
    )
```

time: 469 us -> 59.3 us (0.13)
  waiting for transfers between devices: 388 us -> 0 us
  Pallas kernels: 0 us -> 54.5 us
  matrix products: 23.2 us -> 0 us
  local copies, waits for them, and re-layouts: 23.9 us -> 3.98 us
  between operations: 13.8 us -> 0.64 us
  starting transfers between devices: 12.9 us -> 0 us
  other arithmetic: 7.14 us -> 0 us
    psum x1 -> x0, waiting for transfers between devices: 349 us -> none  [per_device(): gram = lax.psum(partial_value, 'rows')]
    pallas_call x0 -> x1, Pallas kernels: none -> 54.5 us  [per_device(): pl.pallas_call(kernel, out_shape=(jax.ShapeDtypeStruct((SNAPS, 2, NX, NY)...]
    dot_general x2 -> x0, matrix products: 23.2 us -> none  [project(): return jnp.dot(piece, adjoint_flat.T, preferred_element_type=jnp.float32)]
    all_gather x2 -> x0, waiting for transfers between devices: 23.1 us -> none  [the longest x1 20.1 us: per_device(): first = project(lax.all_gather(low_one, 'cols', axis=0, tiled=True))]
    unnamed x8 -> x2, local copies, waits for them, and re-layouts: 22.4 us -> 3.98 us
    ppermute x4 -> x0, waiting for transfers between devices: 15.2 us -> none  [the longest x2 12.4 us: padded_2(): lax.ppermute(tail, axis, [(i, (i + 1) % count) for i in range(count)])]
    ppermute x4 -> x0, starting transfers between devices: 12.6 us -> none  [the longest x2 9.09 us: padded_2(): lax.ppermute(head, axis, [((i + 1) % count, i) for i in range(count)])]
  transfers between devices with their start and end apart: 7 -> 0, of which waited for: 7 -> 0; matrix products, arithmetic and copies ran while one was open for 7% -> 0% of each run, Pallas kernels for 0% -> 0%
where the time goes in v1:
time: 59.3 us; the launch traced here: 59.1 us
  Pallas kernels  54.5 us (92%)
  local copies, waits for them, and re-layouts  3.98 us (7%)
  between operations  0.64 us (1%)
    pallas_call x1, Pallas kernels, per_device(): pl.pallas_call(kernel, out_shape=(jax.ShapeDtypeStruct((SNAPS, 2, NX, NY)...  54.5 us
    unnamed x2, local copies, waits for them, and re-layouts  3.98 us

profile of v1, /device:TPU:0, one launch (start us, length us, event | category | flops | bytes accessed | tf_op | source)
XLA Modules:
  0.0 59.1 jit_solution(11953243276254331798)
XLA Ops:
  0.6 54.5 %shard_map.59 = (f32[16,2,16,512]{3,2,1,0:T(8,128)}, f32[2,64,512]{2,1,0:T(8,128)}) custom-call(f32[16,2,16,512]{3,2,1,0:T(8,128)} %snaps_hbm.1, bf16[512,2,16,512]{3,2,1,0:T(8,128)(2,1)} %adj_hbm.1, f32[1,512]{1,0:T(1,128)} %bitcast.2, f32[1,512]{1,0:T(1,128)} %bitcast.3), custom_call_target="tpu_custom_call" | custom-call | tf_op jit(solution)/shard_map/pallas_call | solution.py:322
  55.1 2.3 %copy.8 = f32[16,2,16,512]{3,2,1,0:T(8,128)} copy(f32[16,2,16,512]{3,2,1,0:T(8,128)} %get-tuple-element.4) | data formatting | bytes 2097152
  57.4 1.7 %copy.9 = f32[2,64,512]{2,1,0:T(8,128)} copy(f32[2,64,512]{2,1,0:T(8,128)} %get-tuple-element.5) | data formatting | bytes 524288

commit v2 on v0

v2 whole, which is shorter than its diff:
```python
import functools

import jax
import jax.numpy as jnp
from jax import lax
from jax.experimental import pallas as pl
from jax.experimental.pallas import tpu as pltpu
from jax.sharding import PartitionSpec as P

ROWS = 32
SNAPS = 16
ADJS = 512
NX = 16
NY = 512
BLOCK = 32
LOADS = ADJS // BLOCK
SCALE = 8192.0
TINY = 1e-37
CUTS = ((2, 6), (8, 4), (12, 4), (16, 2))
OFFSETS = sorted(
    ((dx, dz, dy) for dx in range(4) for dz in range(4) for dy in range(2) if dx or dz or dy),
    key=lambda step: -(min(step[0], 4 - step[0]) + min(step[1], 4 - step[1]) + 2 * step[2]),
)
MESH = pl.DeviceIdType.MESH
NT = (((1,), (1,)), ((), ()))
F32 = jnp.float32
LOW = jnp.bfloat16


def encode(value):
    scaled = value * SCALE
    square = scaled * scaled
    return ((scaled * jnp.abs(scaled)) * (square * (square * square))).astype(LOW)


def decode(code):
    wide = code.astype(F32)
    half = lax.rsqrt(jnp.maximum(jnp.abs(wide), TINY))
    eighth = lax.rsqrt(lax.rsqrt(half))
    return (wide * half) * (eighth * eighth * eighth) * (1.0 / SCALE)


def kernel(
    snaps_hbm, adj_hbm, base_ref, shear_ref,
    adv_hbm, gram_ref,
    snaps, coef, own, own_one, own_adv, adv_out, code, halo_code,
    code_d, code_p, far_d, far_p, one_d, one_p,
    low_own, low_side, low_d, low_p,
    adj_raw, adj, total, part, gather, result,
    io_sem, load_sem, halo_send, halo_recv, far_send, far_recv,
    pass_send, pass_recv, side_send, side_recv, sum_sem,
):
    row = lax.axis_index("rows")
    col = lax.axis_index("cols")
    side = col + 1 - 2 * (col % 2)
    far_col = (col + 2) % 4
    up = (row + 1) % ROWS
    down = (row + ROWS - 1) % ROWS
    here_x, here_z, here_y = row // 8, (row // 2) % 4, row % 2

    def others():
        for dx, dz, dy in OFFSETS:
            yield ((here_x + dx) % 4) * 8 + ((here_z + dz) % 4) * 2 + (here_y + dy) % 2

    def load(i):
        return pltpu.make_async_copy(
            adj_hbm.at[pl.ds(pl.multiple_of(i * BLOCK, BLOCK), BLOCK)],
            adj_raw.at[i],
            load_sem.at[i],
        )

    def send(src, dst, out_sem, in_sem, to_row, to_col):
        return pltpu.make_async_remote_copy(
            src, dst, out_sem, in_sem, device_id=(to_row, to_col), device_id_type=MESH
        )

    snaps_in = pltpu.make_async_copy(snaps_hbm, snaps, io_sem.at[0])
    snaps_in.start()
    for i in range(LOADS):
        load(i).start()

    barrier = pltpu.get_barrier_semaphore()
    for to in others():
        pl.semaphore_signal(barrier, inc=1, device_id=(to, col), device_id_type=MESH)
    for to in ((row, far_col), (row, side), (up, far_col), (down, far_col)):
        pl.semaphore_signal(barrier, inc=1, device_id=to, device_id_type=MESH)

    lane = lax.broadcasted_iota(jnp.int32, (SNAPS, NY), 1)
    base = jnp.broadcast_to(base_ref[...], (SNAPS, NY))
    coef[0] = 0.1 - 0.3 * base
    coef[1] = 0.1 + 0.3 * base
    coef[2] = jnp.where(lane == NY - 1, 0.0, 0.1)
    coef[3] = jnp.where(lane == 0, 0.0, 0.1)
    coef[4] = 0.3 * jnp.broadcast_to(shear_ref[...], (SNAPS, NY))

    snaps_in.wait()
    for c in range(2):
        turned = jnp.swapaxes(snaps[:, c], 0, 1)
        own[pl.ds(2, NX), c] = turned
        code[:, c] = encode(turned)

    pl.semaphore_wait(barrier, ROWS - 1 + 4)

    tail, head = code.at[pl.ds(NX - 2, 2)], code.at[pl.ds(0, 2)]
    halos = [
        send(tail, halo_code.at[pl.ds(0, 2)], halo_send.at[0], halo_recv.at[0], up, col),
        send(head, halo_code.at[pl.ds(2, 2)], halo_send.at[1], halo_recv.at[1], down, col),
        send(tail, code_d.at[pl.ds(0, 2)], halo_send.at[2], halo_recv.at[2], up, far_col),
        send(head, code_d.at[pl.ds(NX + 2, 2)], halo_send.at[3], halo_recv.at[3], down, far_col),
    ]
    fars = [
        send(
            code.at[pl.ds(at - 2, count)], code_d.at[pl.ds(at, count)],
            far_send.at[j], far_recv.at[j], row, far_col,
        )
        for j, (at, count) in enumerate(CUTS)
    ]
    for copy in halos + fars:
        copy.start()

    passes = [
        send(
            code_d.at[pl.ds(at, count)], code_p.at[pl.ds(at, count)],
            pass_send.at[j], pass_recv.at[j], row, side,
        )
        for j, (at, count) in enumerate(CUTS + ((0, 2), (NX + 2, 2)))
    ]

    def turn(i, _):
        load(i).wait()
        for c in range(2):
            block = jnp.swapaxes(adj_raw[i, :, c], 0, 1)
            for x in range(NX):
                adj[2 * x + c, pl.ds(pl.multiple_of(i * BLOCK, BLOCK), BLOCK)] = block[x]
        return 0

    def step(ref, x):
        flow = [ref[x, 0], ref[x, 1]]
        values = []
        for c in range(2):
            here = flow[c]
            value = 0.6 * here + (coef[0] * ref[x + 1, c] + coef[1] * ref[x - 1, c])
            value += coef[2] * pltpu.roll(here, NY - 1, 1) + coef[3] * pltpu.roll(here, 1, 1)
            if c == 0:
                value -= coef[4] * flow[1]
            values.append(value)
        return values

    lax.fori_loop(0, LOADS // 2, turn, 0)

    halos[0].wait_recv()
    halos[1].wait_recv()
    for k in range(2):
        for c in range(2):
            own[k, c] = decode(halo_code[k, c])
            own[NX + 2 + k, c] = decode(halo_code[2 + k, c])

    def own_first(i, _):
        for k in range(3):
            x = 3 * i + k
            values = step(own, x + 1)
            for c in range(2):
                own_one[x, c] = values[c]
        return 0

    lax.fori_loop(0, (NX + 2) // 3, own_first, 0)

    def own_second(i, _):
        for k in range(4):
            x = 4 * i + k
            values = step(own_one, x + 1)
            for c in range(2):
                own_adv[x, c] = values[c]
                low_own[2 * x + c, pl.ds(0, SNAPS)] = own_one[x + 1, c].astype(LOW)
                low_own[2 * x + c, pl.ds(SNAPS, SNAPS)] = values[c].astype(LOW)
        return 0

    lax.fori_loop(0, NX // 4, own_second, 0)
    to_side = send(low_own, low_side, side_send.at[0], side_recv.at[0], row, side)
    to_side.start()

    lax.fori_loop(LOADS // 2, LOADS - 4, turn, 0)
    for k in range(2):
        halos[2 + k].wait_recv()
        passes[4 + k].start()
    fars[0].wait_recv()
    passes[0].start()
    lax.fori_loop(LOADS - 4, LOADS, turn, 0)

    for c in range(2):
        adv_out[:, c] = jnp.swapaxes(own_adv[:, c], 0, 1)
    adv_copy = pltpu.make_async_copy(adv_out, adv_hbm, io_sem.at[1])
    adv_copy.start()

    def states(codes, wide, one, low, j):
        first = 0 if j == 0 else 4 * j + 4
        for k in range(first, 4 * j + 8):
            for c in range(2):
                wide[k, c] = decode(codes[k, c])
        for x in range(0 if j == 0 else 4 * j + 2, 4 * j + 6):
            values = step(wide, x + 1)
            for c in range(2):
                one[x, c] = values[c]
        for x in range(4 * j, 4 * j + 4):
            values = step(one, x + 1)
            for c in range(2):
                low[2 * x + c, pl.ds(0, SNAPS)] = one[x + 1, c].astype(LOW)
                low[2 * x + c, pl.ds(SNAPS, SNAPS)] = values[c].astype(LOW)

    def multiply(at):
        left = jnp.concatenate(
            [
                jnp.concatenate([ref[at + i] for ref in (low_own, low_side, low_d, low_p)], axis=0)
                for i in range(4)
            ],
            axis=1,
        )
        right = jnp.concatenate([adj[at + i] for i in range(4)], axis=1)
        product = lax.dot_general(left, right, NT, preferred_element_type=F32)
        if at == 0:
            total[...] = product
        else:
            total[...] += product

    states(code_d, far_d, one_d, low_d, 0)
    for copy in (passes[4], passes[5], passes[0], to_side):
        copy.wait_recv()
    states(code_p, far_p, one_p, low_p, 0)
    for j in range(1, 4):
        fars[j].wait_recv()
        passes[j].start()
        multiply(8 * j - 8)
        states(code_d, far_d, one_d, low_d, j)
        passes[j].wait_recv()
        multiply(8 * j - 4)
        states(code_p, far_p, one_p, low_p, j)
    multiply(24)
    multiply(28)

    for g in range(8):
        who = (col, side, far_col, (side + 2) % 4)[g // 2]
        for k in range(4):
            part[(4 * (g % 2) + who) * 4 + k] = total[pl.ds(16 * g, 16), pl.ds(128 * k, 128)]

    for to in others():
        send(part.at[to], gather.at[row], sum_sem.at[0], sum_sem.at[1], to, col).start()
    gather[row] = part[row]
    rest = gather.at[pl.ds(0, ROWS - 1)]
    pltpu.make_async_copy(rest, rest, sum_sem.at[1]).wait()
    sums = [gather[t] for t in range(ROWS)]
    while len(sums) > 1:
        sums = [sums[t] + sums[t + 1] for t in range(0, len(sums), 2)]
    result[row] = sums[0]

    for to in others():
        send(result.at[row], result.at[row], sum_sem.at[2], sum_sem.at[3], to, col).start()
    adv_copy.wait()
    for copy in halos + fars + passes + [to_side]:
        copy.wait_send()
    pltpu.make_async_copy(rest, rest, sum_sem.at[0]).wait()
    pltpu.make_async_copy(rest, rest, sum_sem.at[3]).wait()
    for t in range(ROWS):
        at = 16 * (t // 4)
        gram_ref[at // 64, pl.ds(at % 64, 16), pl.ds(128 * (t % 4), 128)] = result[t]
    pltpu.make_async_copy(rest, rest, sum_sem.at[2]).wait()


def per_device(snapshots, adjoint, base_flow, shear):
    vmem = pltpu.VMEM
    return pl.pallas_call(
        kernel,
        out_shape=(
            jax.ShapeDtypeStruct((SNAPS, 2, NX, NY), F32),
            jax.ShapeDtypeStruct((2, 64, ADJS), F32),
        ),
        in_specs=[
            pl.BlockSpec(memory_space=pl.ANY),
            pl.BlockSpec(memory_space=pl.ANY),
            pl.BlockSpec(memory_space=vmem),
            pl.BlockSpec(memory_space=vmem),
        ],
        out_specs=(pl.BlockSpec(memory_space=pl.ANY), pl.BlockSpec(memory_space=vmem)),
        scratch_shapes=[
            vmem((SNAPS, 2, NX, NY), F32),
            vmem((5, SNAPS, NY), F32),
            vmem((NX + 4, 2, SNAPS, NY), F32),
            vmem((NX + 2, 2, SNAPS, NY), F32),
            vmem((NX, 2, SNAPS, NY), F32),
            vmem((SNAPS, 2, NX, NY), F32),
            vmem((NX, 2, SNAPS, NY), LOW),
            vmem((4, 2, SNAPS, NY), LOW),
            vmem((NX + 4, 2, SNAPS, NY), LOW),
            vmem((NX + 4, 2, SNAPS, NY), LOW),
            vmem((NX + 4, 2, SNAPS, NY), F32),
            vmem((NX + 4, 2, SNAPS, NY), F32),
            vmem((NX + 2, 2, SNAPS, NY), F32),
            vmem((NX + 2, 2, SNAPS, NY), F32),
            vmem((2 * NX, 2 * SNAPS, NY), LOW),
            vmem((2 * NX, 2 * SNAPS, NY), LOW),
            vmem((2 * NX, 2 * SNAPS, NY), LOW),
            vmem((2 * NX, 2 * SNAPS, NY), LOW),
            vmem((LOADS, BLOCK, 2, NX, NY), LOW),
            vmem((2 * NX, ADJS, NY), LOW),
            vmem((128, ADJS), F32),
            vmem((ROWS, 16, 128), F32),
            vmem((ROWS, 16, 128), F32),
            vmem((ROWS, 16, 128), F32),
            pltpu.SemaphoreType.DMA((2,)),
            pltpu.SemaphoreType.DMA((LOADS,)),
            pltpu.SemaphoreType.DMA((4,)),
            pltpu.SemaphoreType.DMA((4,)),
            pltpu.SemaphoreType.DMA((4,)),
            pltpu.SemaphoreType.DMA((4,)),
            pltpu.SemaphoreType.DMA((6,)),
            pltpu.SemaphoreType.DMA((6,)),
            pltpu.SemaphoreType.DMA((1,)),
            pltpu.SemaphoreType.DMA((1,)),
            pltpu.SemaphoreType.DMA((4,)),
        ],
        compiler_params=pltpu.CompilerParams(
            collective_id=0, has_side_effects=True, vmem_limit_bytes=60 * 2**20
        ),
    )(snapshots, adjoint, base_flow.reshape(1, NY), shear.reshape(1, NY))


def solution(mesh):
    in_specs = (P("cols", None, "rows", None), P("cols", None, "rows", None), P(), P())
    out_specs = (P("cols", None, "rows", None), P(None, None, "cols"))
    return jax.shard_map(
        per_device, mesh=mesh, in_specs=in_specs, out_specs=out_specs, check_vma=False
    )
```

time: 469 us -> 50.8 us (0.11)
  waiting for transfers between devices: 388 us -> 0 us
  Pallas kernels: 0 us -> 46 us
  matrix products: 23.2 us -> 0 us
  local copies, waits for them, and re-layouts: 23.9 us -> 3.98 us
  between operations: 13.8 us -> 0.64 us
  starting transfers between devices: 12.9 us -> 0 us
  other arithmetic: 7.14 us -> 0 us
    psum x1 -> x0, waiting for transfers between devices: 349 us -> none  [per_device(): gram = lax.psum(partial_value, 'rows')]
    pallas_call x0 -> x1, Pallas kernels: none -> 46 us  [per_device(): pl.pallas_call(kernel, out_shape=(jax.ShapeDtypeStruct((SNAPS, 2, NX, NY)...]
    dot_general x2 -> x0, matrix products: 23.2 us -> none  [project(): return jnp.dot(piece, adjoint_flat.T, preferred_element_type=jnp.float32)]
    all_gather x2 -> x0, waiting for transfers between devices: 23.1 us -> none  [the longest x1 20.1 us: per_device(): first = project(lax.all_gather(low_one, 'cols', axis=0, tiled=True))]
    unnamed x8 -> x2, local copies, waits for them, and re-layouts: 22.4 us -> 3.98 us
    ppermute x4 -> x0, waiting for transfers between devices: 15.2 us -> none  [the longest x2 12.4 us: padded_2(): lax.ppermute(tail, axis, [(i, (i + 1) % count) for i in range(count)])]
    ppermute x4 -> x0, starting transfers between devices: 12.6 us -> none  [the longest x2 9.09 us: padded_2(): lax.ppermute(head, axis, [((i + 1) % count, i) for i in range(count)])]
  transfers between devices with their start and end apart: 7 -> 0, of which waited for: 7 -> 0; matrix products, arithmetic and copies ran while one was open for 7% -> 0% of each run, Pallas kernels for 0% -> 0%
where the time goes in v2:
time: 50.8 us; the launch traced here: 50.6 us
  Pallas kernels  46 us (91%)
  local copies, waits for them, and re-layouts  3.98 us (8%)
  between operations  0.64 us (1%)
    pallas_call x1, Pallas kernels, per_device(): pl.pallas_call(kernel, out_shape=(jax.ShapeDtypeStruct((SNAPS, 2, NX, NY)...  46 us
    unnamed x2, local copies, waits for them, and re-layouts  3.98 us

profile of v2, /device:TPU:0, one launch (start us, length us, event | category | flops | bytes accessed | tf_op | source)
XLA Modules:
  0.0 50.6 jit_solution(1652304295258467650)
XLA Ops:
  0.6 46.0 %shard_map.59 = (f32[16,2,16,512]{3,2,1,0:T(8,128)}, f32[2,64,512]{2,1,0:T(8,128)}) custom-call(f32[16,2,16,512]{3,2,1,0:T(8,128)} %snaps_hbm.1, bf16[512,2,16,512]{3,2,1,0:T(8,128)(2,1)} %adj_hbm.1, f32[1,512]{1,0:T(1,128)} %bitcast.2, f32[1,512]{1,0:T(1,128)} %bitcast.3), custom_call_target="tpu_custom_call" | custom-call | tf_op jit(solution)/shard_map/pallas_call | solution.py:270
  46.6 2.3 %copy.8 = f32[16,2,16,512]{3,2,1,0:T(8,128)} copy(f32[16,2,16,512]{3,2,1,0:T(8,128)} %get-tuple-element.4) | data formatting | bytes 2097152
  48.9 1.7 %copy.9 = f32[2,64,512]{2,1,0:T(8,128)} copy(f32[2,64,512]{2,1,0:T(8,128)} %get-tuple-element.5) | data formatting | bytes 524288

commit v3 on v2

v3 whole, which is shorter than its diff:
```python
import functools

import jax
import jax.numpy as jnp
from jax import lax
from jax.experimental import pallas as pl
from jax.experimental.pallas import tpu as pltpu
from jax.sharding import PartitionSpec as P

ROWS = 32
SNAPS = 16
ADJS = 512
NX = 16
NY = 512
BLOCK = 32
LOADS = ADJS // BLOCK
SCALE = 8192.0
TINY = 1e-37
CUTS = ((16, 2), (2, 2), (4, 4), (8, 4), (12, 2), (14, 2))
OFFSETS = sorted(
    ((dx, dz, dy) for dx in range(4) for dz in range(4) for dy in range(2) if dx or dz or dy),
    key=lambda step: -(min(step[0], 4 - step[0]) + min(step[1], 4 - step[1]) + 2 * step[2]),
)
MESH = pl.DeviceIdType.MESH
NT = (((1,), (1,)), ((), ()))
F32 = jnp.float32
LOW = jnp.bfloat16


def encode(value):
    scaled = value * SCALE
    square = scaled * scaled
    return ((scaled * jnp.abs(scaled)) * (square * (square * square))).astype(LOW)


def decode(code):
    wide = code.astype(F32)
    half = lax.rsqrt(jnp.maximum(jnp.abs(wide), TINY))
    eighth = lax.rsqrt(lax.rsqrt(half))
    return (wide * half) * (eighth * eighth * eighth) * (1.0 / SCALE)


def kernel(
    snaps_hbm, adj_hbm, base_ref, shear_ref,
    adv_hbm, gram_hbm,
    snaps, coef, own, own_one, own_adv, adv_out, code, halo_code,
    code_d, code_p, far_d, far_p, one_d, one_p,
    low_own, low_side, low_d, low_p,
    adj_raw, adj, total, part, gather, result,
    io_sem, load_sem, halo_send, halo_recv, far_send, far_recv,
    pass_send, pass_recv, side_send, side_recv, both_send, both_recv, sum_sem,
):
    row = lax.axis_index("rows")
    col = lax.axis_index("cols")
    side = col + 1 - 2 * (col % 2)
    far_col = (col + 2) % 4
    far_side = (side + 2) % 4
    up = (row + 1) % ROWS
    down = (row + ROWS - 1) % ROWS
    here_x, here_z, here_y = row // 8, (row // 2) % 4, row % 2

    def others():
        for dx, dz, dy in OFFSETS:
            yield ((here_x + dx) % 4) * 8 + ((here_z + dz) % 4) * 2 + (here_y + dy) % 2

    def load(i):
        return pltpu.make_async_copy(
            adj_hbm.at[pl.ds(pl.multiple_of(i * BLOCK, BLOCK), BLOCK)],
            adj_raw.at[i],
            load_sem.at[i],
        )

    def send(src, dst, out_sem, in_sem, to_row, to_col):
        return pltpu.make_async_remote_copy(
            src, dst, out_sem, in_sem, device_id=(to_row, to_col), device_id_type=MESH
        )

    snaps_in = pltpu.make_async_copy(snaps_hbm, snaps, io_sem.at[0])
    snaps_in.start()
    for i in range(LOADS):
        load(i).start()

    barrier = pltpu.get_barrier_semaphore()
    for to in others():
        pl.semaphore_signal(barrier, inc=1, device_id=(to, col), device_id_type=MESH)
    for to in ((row, far_col), (row, side), (row, far_side), (up, far_col), (down, far_col)):
        pl.semaphore_signal(barrier, inc=1, device_id=to, device_id_type=MESH)

    lane = lax.broadcasted_iota(jnp.int32, (SNAPS, NY), 1)
    base = jnp.broadcast_to(base_ref[...], (SNAPS, NY))
    coef[0] = 0.1 - 0.3 * base
    coef[1] = 0.1 + 0.3 * base
    coef[2] = jnp.where(lane == NY - 1, 0.0, 0.1)
    coef[3] = jnp.where(lane == 0, 0.0, 0.1)
    coef[4] = 0.3 * jnp.broadcast_to(shear_ref[...], (SNAPS, NY))

    snaps_in.wait()
    for c in range(2):
        turned = jnp.swapaxes(snaps[:, c], 0, 1)
        own[pl.ds(2, NX), c] = turned
        code[:, c] = encode(turned)

    pl.semaphore_wait(barrier, ROWS - 1 + 5)

    fars = [
        send(
            code.at[pl.ds(at - 2, count)], code_d.at[pl.ds(at, count)],
            far_send.at[j], far_recv.at[j], row, far_col,
        )
        for j, (at, count) in enumerate(CUTS)
    ]
    at, count = CUTS[-1]
    both = send(
        code.at[pl.ds(at - 2, count)], code_p.at[pl.ds(at, count)],
        both_send.at[0], both_recv.at[0], row, far_side,
    )
    halos = [
        send(code.at[pl.ds(NX - 2, 2)], code_d.at[pl.ds(0, 2)],
             halo_send.at[0], halo_recv.at[0], up, far_col),
        send(code.at[pl.ds(0, 2)], code_d.at[pl.ds(NX + 2, 2)],
             halo_send.at[1], halo_recv.at[1], down, far_col),
    ]
    for copy in [fars[0], fars[1]] + halos + fars[2:] + [both]:
        copy.start()
    relays = [
        send(code_d.at[pl.ds(NX, 2)], halo_code.at[pl.ds(0, 2)],
             halo_send.at[2], halo_recv.at[2], up, far_col),
        send(code_d.at[pl.ds(2, 2)], halo_code.at[pl.ds(2, 2)],
             halo_send.at[3], halo_recv.at[3], down, far_col),
    ]
    passes = [
        send(
            code_d.at[pl.ds(at, count)], code_p.at[pl.ds(at, count)],
            pass_send.at[j], pass_recv.at[j], row, side,
        )
        for j, (at, count) in enumerate(CUTS[:-1] + ((0, 2), (NX + 2, 2)))
    ]

    def turn(i, _):
        load(i).wait()
        for c in range(2):
            block = jnp.swapaxes(adj_raw[i, :, c], 0, 1)
            for x in range(NX):
                adj[2 * x + c, pl.ds(pl.multiple_of(i * BLOCK, BLOCK), BLOCK)] = block[x]
        return 0

    def step(ref, x):
        flow = [ref[x, 0], ref[x, 1]]
        values = []
        for c in range(2):
            here = flow[c]
            value = 0.6 * here + (coef[0] * ref[x + 1, c] + coef[1] * ref[x - 1, c])
            value += coef[2] * pltpu.roll(here, NY - 1, 1) + coef[3] * pltpu.roll(here, 1, 1)
            if c == 0:
                value -= coef[4] * flow[1]
            values.append(value)
        return values

    def own_first(x):
        values = step(own, x + 1)
        for c in range(2):
            own_one[x, c] = values[c]

    def own_second(x):
        values = step(own_one, x + 1)
        for c in range(2):
            own_adv[x, c] = values[c]
            low_own[2 * x + c, pl.ds(0, SNAPS)] = own_one[x + 1, c].astype(LOW)
            low_own[2 * x + c, pl.ds(SNAPS, SNAPS)] = values[c].astype(LOW)

    def inner_first(i, _):
        for k in range(2):
            own_first(2 * i + k)
        return 0

    def inner_second(i, _):
        for k in range(4):
            own_second(2 + 4 * i + k)
        return 0

    lax.fori_loop(1, NX // 2, inner_first, 0)
    lax.fori_loop(0, 3, inner_second, 0)
    to_side = [
        send(low_own.at[pl.ds(at, count)], low_side.at[pl.ds(at, count)],
             side_send.at[j], side_recv.at[j], row, side)
        for j, (at, count) in enumerate(((4, 24), (0, 4), (28, 4)))
    ]
    to_side[0].start()

    lax.fori_loop(0, 5, turn, 0)
    for k in range(2):
        fars[k].wait_recv()
        relays[k].start()
        passes[k].start()
        lax.fori_loop(5 + 2 * k, 7 + 2 * k, turn, 0)
    for k in range(2):
        halos[k].wait_recv()
        passes[5 + k].start()
    lax.fori_loop(9, LOADS, turn, 0)

    relays[0].wait_recv()
    relays[1].wait_recv()
    for k in range(2):
        for c in range(2):
            own[k, c] = decode(halo_code[k, c])
            own[NX + 2 + k, c] = decode(halo_code[2 + k, c])
    for x in (0, 1, NX, NX + 1):
        own_first(x)
    for x in (0, 1, NX - 2, NX - 1):
        own_second(x)
    to_side[1].start()
    to_side[2].start()

    fars[2].wait_recv()
    passes[2].start()
    for c in range(2):
        adv_out[:, c] = jnp.swapaxes(own_adv[:, c], 0, 1)
    adv_copy = pltpu.make_async_copy(adv_out, adv_hbm, io_sem.at[1])
    adv_copy.start()

    def states(refs, codes, firsts, seconds):
        code_ref, wide, one, low = refs
        for k in codes:
            for c in range(2):
                wide[k, c] = decode(code_ref[k, c])
        for x in firsts:
            values = step(wide, x + 1)
            for c in range(2):
                one[x, c] = values[c]
        for x in seconds:
            values = step(one, x + 1)
            for c in range(2):
                low[2 * x + c, pl.ds(0, SNAPS)] = one[x + 1, c].astype(LOW)
                low[2 * x + c, pl.ds(SNAPS, SNAPS)] = values[c].astype(LOW)

    direct = (code_d, far_d, one_d, low_d)
    passed = (code_p, far_p, one_p, low_p)

    def multiply(at):
        left = jnp.concatenate(
            [
                jnp.concatenate([ref[at + i] for ref in (low_own, low_side, low_d, low_p)], axis=0)
                for i in range(4)
            ],
            axis=1,
        )
        right = jnp.concatenate([adj[at + i] for i in range(4)], axis=1)
        product = lax.dot_general(left, right, NT, preferred_element_type=F32)
        if at == 4:
            total[...] = product
        else:
            total[...] += product

    states(direct, range(8), range(6), range(4))
    for copy in (passes[5], passes[1], passes[2]):
        copy.wait_recv()
    states(passed, range(8), range(6), range(4))

    to_side[0].wait_recv()
    fars[3].wait_recv()
    passes[3].start()
    multiply(4)
    states(direct, range(8, 12), range(6, 10), range(4, 8))
    passes[3].wait_recv()
    to_side[1].wait_recv()
    multiply(0)
    states(passed, range(8, 12), range(6, 10), range(4, 8))

    fars[4].wait_recv()
    passes[4].start()
    for copy in (passes[0], passes[6]):
        copy.wait_recv()
    multiply(8)
    states(direct, (12, 13, 16, 17, 18, 19), (10, 11, 16, 17), (8, 9))
    passes[4].wait_recv()
    multiply(12)
    states(passed, (12, 13, 16, 17, 18, 19), (10, 11, 16, 17), (8, 9))

    fars[5].wait_recv()
    multiply(16)
    states(direct, (14, 15), range(12, 16), range(10, 16))
    both.wait_recv()
    to_side[2].wait_recv()
    states(passed, (14, 15), range(12, 16), range(10, 16))
    multiply(20)
    multiply(24)
    multiply(28)

    for g in range(8):
        who = (col, side, far_col, far_side)[g // 2]
        for k in range(4):
            part[(4 * (g % 2) + who) * 4 + k] = total[pl.ds(16 * g, 16), pl.ds(128 * k, 128)]

    for to in others():
        send(part.at[to], gather.at[row], sum_sem.at[0], sum_sem.at[1], to, col).start()
    gather[row] = part[row]
    rest = gather.at[pl.ds(0, ROWS - 1)]
    pltpu.make_async_copy(rest, rest, sum_sem.at[1]).wait()
    sums = [gather[t] for t in range(ROWS)]
    while len(sums) > 1:
        sums = [sums[t] + sums[t + 1] for t in range(0, len(sums), 2)]
    result[...] = sums[0]

    place = gram_hbm.at[
        row // 16,
        pl.ds(pl.multiple_of((row // 4) % 4 * 16, 16), 16),
        pl.ds(pl.multiple_of(row % 4 * 128, 128), 128),
    ]
    for to in others():
        send(result, place, sum_sem.at[2], sum_sem.at[3], to, col).start()
    own_piece = pltpu.make_async_copy(result, place, io_sem.at[0])
    own_piece.start()
    adv_copy.wait()
    for copy in halos + fars + relays + passes + to_side + [both]:
        copy.wait_send()
    own_piece.wait()
    pltpu.make_async_copy(rest, rest, sum_sem.at[0]).wait()
    pltpu.make_async_copy(rest, rest, sum_sem.at[2]).wait()
    pltpu.make_async_copy(rest, rest, sum_sem.at[3]).wait()


def hand_on(adv_in, gram_in, adv_hbm, gram_hbm, adv, gram, in_sem, out_sem):
    ways = [(adv_in.at[pl.ds(4 * i, 4)], adv.at[pl.ds(4 * i, 4)], adv_hbm.at[pl.ds(4 * i, 4)]) for i in range(4)]
    ways += [(gram_in.at[i], gram.at[i], gram_hbm.at[i]) for i in range(2)]
    for i, (src, mid, _) in enumerate(ways):
        pltpu.make_async_copy(src, mid, in_sem.at[i]).start()
    for i, (src, mid, dst) in enumerate(ways):
        pltpu.make_async_copy(src, mid, in_sem.at[i]).wait()
        pltpu.make_async_copy(mid, dst, out_sem.at[i]).start()
    for i, (_, mid, dst) in enumerate(ways):
        pltpu.make_async_copy(mid, dst, out_sem.at[i]).wait()


def per_device(snapshots, adjoint, base_flow, shear):
    vmem = pltpu.VMEM
    somewhere = pl.BlockSpec(memory_space=pl.ANY)
    shapes = (
        jax.ShapeDtypeStruct((SNAPS, 2, NX, NY), F32),
        jax.ShapeDtypeStruct((2, 64, ADJS), F32),
    )
    results = pl.pallas_call(
        kernel,
        out_shape=shapes,
        in_specs=[
            somewhere,
            somewhere,
            pl.BlockSpec(memory_space=vmem),
            pl.BlockSpec(memory_space=vmem),
        ],
        out_specs=(somewhere, somewhere),
        scratch_shapes=[
            vmem((SNAPS, 2, NX, NY), F32),
            vmem((5, SNAPS, NY), F32),
            vmem((NX + 4, 2, SNAPS, NY), F32),
            vmem((NX + 2, 2, SNAPS, NY), F32),
            vmem((NX, 2, SNAPS, NY), F32),
            vmem((SNAPS, 2, NX, NY), F32),
            vmem((NX, 2, SNAPS, NY), LOW),
            vmem((4, 2, SNAPS, NY), LOW),
            vmem((NX + 4, 2, SNAPS, NY), LOW),
            vmem((NX + 4, 2, SNAPS, NY), LOW),
            vmem((NX + 4, 2, SNAPS, NY), F32),
            vmem((NX + 4, 2, SNAPS, NY), F32),
            vmem((NX + 2, 2, SNAPS, NY), F32),
            vmem((NX + 2, 2, SNAPS, NY), F32),
            vmem((2 * NX, 2 * SNAPS, NY), LOW),
            vmem((2 * NX, 2 * SNAPS, NY), LOW),
            vmem((2 * NX, 2 * SNAPS, NY), LOW),
            vmem((2 * NX, 2 * SNAPS, NY), LOW),
            vmem((LOADS, BLOCK, 2, NX, NY), LOW),
            vmem((2 * NX, ADJS, NY), LOW),
            vmem((128, ADJS), F32),
            vmem((ROWS, 16, 128), F32),
            vmem((ROWS, 16, 128), F32),
            vmem((16, 128), F32),
            pltpu.SemaphoreType.DMA((2,)),
            pltpu.SemaphoreType.DMA((LOADS,)),
            pltpu.SemaphoreType.DMA((4,)),
            pltpu.SemaphoreType.DMA((4,)),
            pltpu.SemaphoreType.DMA((6,)),
            pltpu.SemaphoreType.DMA((6,)),
            pltpu.SemaphoreType.DMA((7,)),
            pltpu.SemaphoreType.DMA((7,)),
            pltpu.SemaphoreType.DMA((3,)),
            pltpu.SemaphoreType.DMA((3,)),
            pltpu.SemaphoreType.DMA((1,)),
            pltpu.SemaphoreType.DMA((1,)),
            pltpu.SemaphoreType.DMA((4,)),
        ],
        compiler_params=pltpu.CompilerParams(
            collective_id=0, has_side_effects=True, vmem_limit_bytes=60 * 2**20
        ),
    )(snapshots, adjoint, base_flow.reshape(1, NY), shear.reshape(1, NY))
    return pl.pallas_call(
        hand_on,
        out_shape=shapes,
        in_specs=[somewhere, somewhere],
        out_specs=(somewhere, somewhere),
        scratch_shapes=[
            vmem((SNAPS, 2, NX, NY), F32),
            vmem((2, 64, ADJS), F32),
            pltpu.SemaphoreType.DMA((6,)),
            pltpu.SemaphoreType.DMA((6,)),
        ],
    )(*results)


def solution(mesh):
    in_specs = (P("cols", None, "rows", None), P("cols", None, "rows", None), P(), P())
    out_specs = (P("cols", None, "rows", None), P(None, None, "cols"))
    return jax.shard_map(
        per_device, mesh=mesh, in_specs=in_specs, out_specs=out_specs, check_vma=False
    )
```

time: 50.8 us -> 46.5 us (0.915)
  local copies, waits for them, and re-layouts: 3.98 us -> 0 us
    unnamed x2 -> x0, local copies, waits for them, and re-layouts: 3.98 us -> none
    pallas_call x1 -> x2, Pallas kernels: 46 us -> 45.7 us  [the longest x1 43.6 us: per_device(): pl.pallas_call(kernel, out_shape=shapes, in_specs=[somewhere, somewhere,...]
where the time goes in v3:
time: 46.5 us; the launch traced here: 46.3 us
  Pallas kernels  45.7 us (98%)
  between operations  0.64 us (1%)
    pallas_call x1, Pallas kernels, per_device(): pl.pallas_call(kernel, out_shape=shapes, in_specs=[somewhere, somewhere,...  43.6 us
    pallas_call x1, Pallas kernels, per_device(): pl.pallas_call(hand_on, out_shape=shapes, in_specs=[somewhere, somewhere]...  2.1 us

profile of v3, /device:TPU:0, one launch (start us, length us, event | category | flops | bytes accessed | tf_op | source)
XLA Modules:
  0.0 46.3 jit_solution(11324964603612228381)
XLA Ops:
  0.6 43.6 %shard_map.59 = (f32[16,2,16,512]{3,2,1,0:T(8,128)}, f32[2,64,512]{2,1,0:T(8,128)}) custom-call(f32[16,2,16,512]{3,2,1,0:T(8,128)} %snaps_hbm.1, bf16[512,2,16,512]{3,2,1,0:T(8,128)(2,1)} %adj_hbm.1, f32[1,512]{1,0:T(1,128)} %bitcast.2, f32[1,512]{1,0:T(1,128)} %bitcast.3), custom_call_target="tpu_custom_call" | custom-call | tf_op jit(solution)/shard_map/pallas_call | solution.py:341
  44.2 2.1 %shard_map.60 = (f32[16,2,16,512]{3,2,1,0:T(8,128)}, f32[2,64,512]{2,1,0:T(8,128)}) custom-call(f32[16,2,16,512]{3,2,1,0:T(8,128)} %get-tuple-element.4.adv_in, f32[2,64,512]{2,1,0:T(8,128)} %get-tuple-element.5.gram_in), custom_call_target="tpu_custom_call" | custom-call | tf_op jit(solution)/shard_map/pallas_call | solution.py:394

commit v4 on v3

--- a/solution.py
+++ b/solution.py
@@ -14,6 +14,7 @@
 NY = 512
 BLOCK = 32
 LOADS = ADJS // BLOCK
+TURNED = 20
 SCALE = 8192.0
 TINY = 1e-37
 CUTS = ((16, 2), (2, 2), (4, 4), (8, 4), (12, 2), (14, 2))
@@ -46,7 +47,7 @@
     snaps, coef, own, own_one, own_adv, adv_out, code, halo_code,
     code_d, code_p, far_d, far_p, one_d, one_p,
     low_own, low_side, low_d, low_p,
-    adj_raw, adj, total, part, gather, result,
+    adj_raw, adj, adj_t, total, part, gather, result,
     io_sem, load_sem, halo_send, halo_recv, far_send, far_recv,
     pass_send, pass_recv, side_send, side_recv, both_send, both_recv, sum_sem,
 ):
@@ -77,8 +78,6 @@
 
     snaps_in = pltpu.make_async_copy(snaps_hbm, snaps, io_sem.at[0])
     snaps_in.start()
-    for i in range(LOADS):
-        load(i).start()
 
     barrier = pltpu.get_barrier_semaphore()
     for to in others():
@@ -95,6 +94,8 @@
     coef[4] = 0.3 * jnp.broadcast_to(shear_ref[...], (SNAPS, NY))
 
     snaps_in.wait()
+    for i in range(LOADS):
+        load(i).start()
     for c in range(2):
         turned = jnp.swapaxes(snaps[:, c], 0, 1)
         own[pl.ds(2, NX), c] = turned
@@ -143,6 +144,15 @@
             for x in range(NX):
                 adj[2 * x + c, pl.ds(pl.multiple_of(i * BLOCK, BLOCK), BLOCK)] = block[x]
         return 0
+
+    def turn_group(g):
+        lax.fori_loop(4 * g, 4 * g + 4, turn, 0)
+
+        def turn_round(k, _):
+            adj_t[k, :, pl.ds(128 * g, 128)] = adj[TURNED + k, pl.ds(128 * g, 128)].T
+            return 0
+
+        lax.fori_loop(0, 2 * NX - TURNED, turn_round, 0)
 
     def step(ref, x):
         flow = [ref[x, 0], ref[x, 1]]
@@ -187,36 +197,19 @@
     ]
     to_side[0].start()
 
-    lax.fori_loop(0, 5, turn, 0)
+    turn_group(0)
     for k in range(2):
         fars[k].wait_recv()
         relays[k].start()
         passes[k].start()
-        lax.fori_loop(5 + 2 * k, 7 + 2 * k, turn, 0)
+    turn_group(1)
     for k in range(2):
         halos[k].wait_recv()
         passes[5 + k].start()
-    lax.fori_loop(9, LOADS, turn, 0)
-
-    relays[0].wait_recv()
-    relays[1].wait_recv()
-    for k in range(2):
-        for c in range(2):
-            own[k, c] = decode(halo_code[k, c])
-            own[NX + 2 + k, c] = decode(halo_code[2 + k, c])
-    for x in (0, 1, NX, NX + 1):
-        own_first(x)
-    for x in (0, 1, NX - 2, NX - 1):
-        own_second(x)
-    to_side[1].start()
-    to_side[2].start()
-
+    turn_group(2)
     fars[2].wait_recv()
     passes[2].start()
-    for c in range(2):
-        adv_out[:, c] = jnp.swapaxes(own_adv[:, c], 0, 1)
-    adv_copy = pltpu.make_async_copy(adv_out, adv_hbm, io_sem.at[1])
-    adv_copy.start()
+    turn_group(3)
 
     def states(refs, codes, firsts, seconds):
         code_ref, wide, one, low = refs
@@ -236,38 +229,53 @@
     direct = (code_d, far_d, one_d, low_d)
     passed = (code_p, far_p, one_p, low_p)
 
-    def multiply(at):
+    def multiply(at, count=4):
         left = jnp.concatenate(
             [
                 jnp.concatenate([ref[at + i] for ref in (low_own, low_side, low_d, low_p)], axis=0)
-                for i in range(4)
+                for i in range(count)
             ],
             axis=1,
         )
-        right = jnp.concatenate([adj[at + i] for i in range(4)], axis=1)
-        product = lax.dot_general(left, right, NT, preferred_element_type=F32)
+        if at < TURNED:
+            right = jnp.concatenate([adj[at + i] for i in range(count)], axis=1)
+            product = lax.dot_general(left, right, NT, preferred_element_type=F32)
+        else:
+            right = adj_t[pl.ds(at - TURNED, count)].reshape(count * NY, ADJS)
+            product = jnp.dot(left, right, preferred_element_type=F32)
         if at == 4:
             total[...] = product
         else:
             total[...] += product
 
     states(direct, range(8), range(6), range(4))
+    fars[3].wait_recv()
+    passes[3].start()
     for copy in (passes[5], passes[1], passes[2]):
         copy.wait_recv()
     states(passed, range(8), range(6), range(4))
+    fars[4].wait_recv()
+    passes[4].start()
+
+    relays[0].wait_recv()
+    relays[1].wait_recv()
+    for k in range(2):
+        for c in range(2):
+            own[k, c] = decode(halo_code[k, c])
+            own[NX + 2 + k, c] = decode(halo_code[2 + k, c])
+    for x in (0, 1, NX, NX + 1):
+        own_first(x)
+    for x in (0, 1, NX - 2, NX - 1):
+        own_second(x)
+    to_side[1].start()
+    to_side[2].start()
 
     to_side[0].wait_recv()
-    fars[3].wait_recv()
-    passes[3].start()
     multiply(4)
     states(direct, range(8, 12), range(6, 10), range(4, 8))
     passes[3].wait_recv()
-    to_side[1].wait_recv()
-    multiply(0)
     states(passed, range(8, 12), range(6, 10), range(4, 8))
 
-    fars[4].wait_recv()
-    passes[4].start()
     for copy in (passes[0], passes[6]):
         copy.wait_recv()
     multiply(8)
@@ -275,6 +283,8 @@
     passes[4].wait_recv()
     multiply(12)
     states(passed, (12, 13, 16, 17, 18, 19), (10, 11, 16, 17), (8, 9))
+    to_side[1].wait_recv()
+    multiply(0)
 
     fars[5].wait_recv()
     multiply(16)
@@ -282,9 +292,7 @@
     both.wait_recv()
     to_side[2].wait_recv()
     states(passed, (14, 15), range(12, 16), range(10, 16))
-    multiply(20)
-    multiply(24)
-    multiply(28)
+    multiply(20, 12)
 
     for g in range(8):
         who = (col, side, far_col, far_side)[g // 2]
@@ -294,6 +302,10 @@
     for to in others():
         send(part.at[to], gather.at[row], sum_sem.at[0], sum_sem.at[1], to, col).start()
     gather[row] = part[row]
+    for c in range(2):
+        adv_out[:, c] = jnp.swapaxes(own_adv[:, c], 0, 1)
+    adv_copy = pltpu.make_async_copy(adv_out, adv_hbm, io_sem.at[1])
+    adv_copy.start()
     rest = gather.at[pl.ds(0, ROWS - 1)]
     pltpu.make_async_copy(rest, rest, sum_sem.at[1]).wait()
     sums = [gather[t] for t in range(ROWS)]
@@ -369,6 +381,7 @@
             vmem((2 * NX, 2 * SNAPS, NY), LOW),
             vmem((LOADS, BLOCK, 2, NX, NY), LOW),
             vmem((2 * NX, ADJS, NY), LOW),
+            vmem((2 * NX - TURNED, NY, ADJS), LOW),
             vmem((128, ADJS), F32),
             vmem((ROWS, 16, 128), F32),
             vmem((ROWS, 16, 128), F32),

time: 46.5 us -> 43.9 us (0.944)
  Pallas kernels: 45.7 us -> 43 us
    pallas_call x1, Pallas kernels: 43.6 us -> 40.9 us  [per_device(): pl.pallas_call(kernel, out_shape=shapes, in_specs=[somewhere, somewhere,...]
where the time goes in v4:
time: 43.9 us; the launch traced here: 43.7 us
  Pallas kernels  43 us (98%)
  between operations  0.64 us (1%)
    pallas_call x1, Pallas kernels, per_device(): pl.pallas_call(kernel, out_shape=shapes, in_specs=[somewhere, somewhere,...  40.9 us
    pallas_call x1, Pallas kernels, per_device(): pl.pallas_call(hand_on, out_shape=shapes, in_specs=[somewhere, somewhere]...  2.1 us

profile of v4, /device:TPU:0, one launch (start us, length us, event | category | flops | bytes accessed | tf_op | source)
XLA Modules:
  0.0 43.7 jit_solution(1923915111366856676)
XLA Ops:
  0.6 40.9 %shard_map.59 = (f32[16,2,16,512]{3,2,1,0:T(8,128)}, f32[2,64,512]{2,1,0:T(8,128)}) custom-call(f32[16,2,16,512]{3,2,1,0:T(8,128)} %snaps_hbm.1, bf16[512,2,16,512]{3,2,1,0:T(8,128)(2,1)} %adj_hbm.1, f32[1,512]{1,0:T(1,128)} %bitcast.2, f32[1,512]{1,0:T(1,128)} %bitcast.3), custom_call_target="tpu_custom_call" | custom-call | tf_op jit(solution)/shard_map/pallas_call | solution.py:353
  41.6 2.1 %shard_map.60 = (f32[16,2,16,512]{3,2,1,0:T(8,128)}, f32[2,64,512]{2,1,0:T(8,128)}) custom-call(f32[16,2,16,512]{3,2,1,0:T(8,128)} %get-tuple-element.4.adv_in, f32[2,64,512]{2,1,0:T(8,128)} %get-tuple-element.5.gram_in), custom_call_target="tpu_custom_call" | custom-call | tf_op jit(solution)/shard_map/pallas_call | solution.py:407

commit v5 on v4

--- a/solution.py
+++ b/solution.py
@@ -14,7 +14,7 @@
 NY = 512
 BLOCK = 32
 LOADS = ADJS // BLOCK
-TURNED = 20
+TURNED = 24
 SCALE = 8192.0
 TINY = 1e-37
 CUTS = ((16, 2), (2, 2), (4, 4), (8, 4), (12, 2), (14, 2))
@@ -76,8 +76,12 @@
             src, dst, out_sem, in_sem, device_id=(to_row, to_col), device_id_type=MESH
         )
 
-    snaps_in = pltpu.make_async_copy(snaps_hbm, snaps, io_sem.at[0])
-    snaps_in.start()
+    snaps_in = [
+        pltpu.make_async_copy(snaps_hbm.at[:, pl.ds(c, 1)], snaps.at[:, pl.ds(c, 1)], io_sem.at[c])
+        for c in range(2)
+    ]
+    for copy in snaps_in:
+        copy.start()
 
     barrier = pltpu.get_barrier_semaphore()
     for to in others():
@@ -93,10 +97,11 @@
     coef[3] = jnp.where(lane == 0, 0.0, 0.1)
     coef[4] = 0.3 * jnp.broadcast_to(shear_ref[...], (SNAPS, NY))
 
-    snaps_in.wait()
-    for i in range(LOADS):
-        load(i).start()
     for c in range(2):
+        snaps_in[c].wait()
+        if c == 1:
+            for i in range(LOADS):
+                load(i).start()
         turned = jnp.swapaxes(snaps[:, c], 0, 1)
         own[pl.ds(2, NX), c] = turned
         code[:, c] = encode(turned)
@@ -292,7 +297,8 @@
     both.wait_recv()
     to_side[2].wait_recv()
     states(passed, (14, 15), range(12, 16), range(10, 16))
-    multiply(20, 12)
+    multiply(20)
+    multiply(24, 8)
 
     for g in range(8):
         who = (col, side, far_col, far_side)[g // 2]

time: 43.9 us -> 43.7 us (level)
  no operation moved by 1% of the time
where the time goes in v5:
time: 43.7 us; the launch traced here: 43.5 us
  Pallas kernels  42.9 us (98%)
  between operations  0.64 us (1%)
    pallas_call x1, Pallas kernels, per_device(): pl.pallas_call(kernel, out_shape=shapes, in_specs=[somewhere, somewhere,...  40.8 us
    pallas_call x1, Pallas kernels, per_device(): pl.pallas_call(hand_on, out_shape=shapes, in_specs=[somewhere, somewhere]...  2.1 us

profile of v5, /device:TPU:0, one launch (start us, length us, event | category | flops | bytes accessed | tf_op | source)
XLA Modules:
  0.0 43.5 jit_solution(8982870811654417463)
XLA Ops:
  0.6 40.8 %shard_map.59 = (f32[16,2,16,512]{3,2,1,0:T(8,128)}, f32[2,64,512]{2,1,0:T(8,128)}) custom-call(f32[16,2,16,512]{3,2,1,0:T(8,128)} %snaps_hbm.1, bf16[512,2,16,512]{3,2,1,0:T(8,128)(2,1)} %adj_hbm.1, f32[1,512]{1,0:T(1,128)} %bitcast.2, f32[1,512]{1,0:T(1,128)} %bitcast.3), custom_call_target="tpu_custom_call" | custom-call | tf_op jit(solution)/shard_map/pallas_call | solution.py:359
  41.4 2.1 %shard_map.60 = (f32[16,2,16,512]{3,2,1,0:T(8,128)}, f32[2,64,512]{2,1,0:T(8,128)}) custom-call(f32[16,2,16,512]{3,2,1,0:T(8,128)} %get-tuple-element.4.adv_in, f32[2,64,512]{2,1,0:T(8,128)} %get-tuple-element.5.gram_in), custom_call_target="tpu_custom_call" | custom-call | tf_op jit(solution)/shard_map/pallas_call | solution.py:413
